TPU v7x, 32 devices: a whole 2x2x4 slice. The times are simulated.
32 devices in a mesh: grp: 2 (over y), shot: 16 (over z, x, core), depth: 1.
Axes of the slice: x: 2, y: 2, z: 4, core: 2. Of those that a mesh axis runs over, the one named last changes fastest.
Arguments:
- velocity_p: bfloat16 [128, 8, 8, 128], P(('grp', 'shot'), None, None, 'depth'), parts along dimension 0, may hold values from 0.5 to 0.8984375
- velocity_s: bfloat16 [128, 8, 8, 128], P(('grp', 'shot'), None, None, 'depth'), parts along dimension 0, may hold values from 0.19921875 to 0.5
- density: bfloat16 [128, 8, 8, 128], P(('grp', 'shot'), None, None, 'depth'), parts along dimension 0, may hold values from 1 to 2
- perturbation: bfloat16 [128, 8, 8, 128], P(('grp', 'shot'), None, None, 'depth'), parts along dimension 0, may hold values from -4 to 4
- seafloor: int32 [128, 8, 8], P(('grp', 'shot')), parts along dimension 0, may hold values from 16 to 63
- owner_ids: int32 [128], P(('grp', 'shot')), parts along dimension 0, may hold values from 0 to 63, each once
- corner_x: int32 [32], P(('grp', 'shot')), parts along dimension 0, may hold values from 0 to 4
- corner_y: int32 [32], P(('grp', 'shot')), parts along dimension 0, may hold values from 0 to 4
- wave_prev: bfloat16 [32, 32, 32, 128], P(('grp', 'shot'), None, None, 'depth'), parts along dimension 0, may hold values from -6 to 6
- wave_now: bfloat16 [32, 32, 32, 128], P(('grp', 'shot'), None, None, 'depth'), parts along dimension 0, may hold values from -6 to 6
Outputs:
- hessian_vec: float32 [128, 8, 8, 128], P(('grp', 'shot'), None, None, 'depth'), parts along dimension 0
There are 2 independent parts, one for each index of `grp`. A program takes and returns all parts, laid end to end along the dimension named above; each array names one. Nothing has to cross between parts.
Inputs may be any that keep to these rules, and one draw needn't show every extreme that they name: `owner_ids`: each lateral block is held by exactly one slot. Shot s images the block rows corner_x[s] to corner_x[s] + 3. Shot s images the block columns corner_y[s] to corner_y[s] + 3.
All inputs are finite; a program needn't handle non-finite values.
Results may differ from a plain program's by a relative error of at most 0.0048.
Values may be sent and summed in bfloat16 or wider, within the bound.
No kernel may reach another device: no remote copies, remote signals or barrier semaphores. Data moves between devices by JAX's collectives and lax.ppermute only.
A program may use at most 64 MiB of HBM per device.

v0:
```python
import functools

import jax
import jax.numpy as jnp
from jax import lax
from jax.experimental import pallas as pl
from jax.experimental.pallas import tpu as pltpu
from jax.sharding import PartitionSpec as P

APX = 4
APY = 4
STEPS = 4
GRID_COLS = 8
NEAR = 4
LANES = 8

speed_factor = 0.28
image_scale = 0.01


def with_halo(block, sides, width):
    for axis, dim in sides:
        count = lax.axis_size(axis)
        forward = [(i, i + 1) for i in range(count - 1)]
        backward = [(target, source) for source, target in forward]
        low = lax.ppermute(
            lax.slice_in_dim(block, block.shape[dim] - width, None, axis=dim), axis, forward
        )
        high = lax.ppermute(lax.slice_in_dim(block, 0, width, axis=dim), axis, backward)
        block = jnp.concatenate([low, block, high], axis=dim)
    return block


def laplace_many(fields):
    stacked = jnp.stack(fields)
    padded = with_halo(stacked.astype(jnp.bfloat16), (("depth", 3),), 1).astype(stacked.dtype)
    padded = jnp.pad(padded, ((0, 0), (1, 1), (1, 1), (0, 0)))
    beside = padded[:, 2:, 1:-1, 1:-1] + padded[:, :-2, 1:-1, 1:-1]
    beside = beside + padded[:, 1:-1, 2:, 1:-1] + padded[:, 1:-1, :-2, 1:-1]
    beside = beside + padded[:, 1:-1, 1:-1, 2:] + padded[:, 1:-1, 1:-1, :-2]
    result = beside - 6.0 * stacked
    return [result[index] for index in range(len(fields))]


def propagate(kappa, contrast, before, current, apply):
    grads = []
    datas = []
    grad_now = apply([current])[0]
    delta_prev = jnp.zeros_like(current)
    delta_now = contrast * grad_now
    grads.append(grad_now)
    datas.append(delta_now)
    before, current = (current, 2.0 * current - before + kappa * grad_now)
    for step in range(1, STEPS):
        grad_now, spread = apply([current, delta_now])
        delta_next = 2.0 * delta_now - delta_prev + kappa * spread + contrast * grad_now
        grads.append(grad_now)
        datas.append(delta_next)
        delta_prev, delta_now = (delta_now, delta_next)
        if step + 1 < STEPS:
            before, current = (current, 2.0 * current - before + kappa * grad_now)
    back = datas[STEPS - 1]
    back_after = jnp.zeros_like(back)
    image = grads[STEPS - 1] * back
    for step in range(STEPS - 2, -1, -1):
        spread = apply([kappa * back])
        back_new = 2.0 * back - back_after + spread[0] + datas[step]
        image = image + grads[step] * back_new
        back_after, back = (back, back_new)
    return image


def vmem():
    return pl.BlockSpec(memory_space=pltpu.VMEM)


def smem():
    return pl.BlockSpec(memory_space=pltpu.SMEM)


def prepare_kernel(
    ids_ref, row_ref, col_ref, floor_ref, p_ref, s_ref, rho_ref, pert_ref, out_ref
):
    slots, block_x, block_y, depth = p_ref.shape
    shape = (block_y, depth)
    deep = lax.broadcasted_iota(jnp.int32, shape, 1).astype(jnp.float32)
    near = lax.broadcasted_iota(jnp.int32, (block_y, block_y), 0) == (
        lax.broadcasted_iota(jnp.int32, (block_y, block_y), 1)
    )
    for slot in range(slots):
        floors = floor_ref[slot].astype(jnp.float32)
        for x in range(block_x):
            line = jnp.broadcast_to(floors[x:x + 1], (block_y, block_y))
            floor = jnp.sum(jnp.where(near, line, 0.0), axis=1, keepdims=True)
            primary = p_ref[slot, x].astype(jnp.float32)
            shear = s_ref[slot, x].astype(jnp.float32)
            square = primary * primary
            stiffness = jnp.where(deep >= floor, square + shear * shear, square)
            coef = speed_factor * stiffness / rho_ref[slot, x].astype(jnp.float32)
            out_ref[2 * x, slot] = coef.astype(out_ref.dtype)
            out_ref[2 * x + 1, slot] = pert_ref[slot, x]
    lane = lax.broadcasted_iota(jnp.int32, shape, 1)
    facts = jnp.where(lane == slots, row_ref[0], 0)
    facts = jnp.where(lane == slots + 1, col_ref[0], facts)
    for slot in range(slots):
        facts = jnp.where(lane == slot, ids_ref[slot], facts)
    facts = facts.astype(jnp.float32).astype(out_ref.dtype)
    for piece in range(out_ref.shape[0]):
        out_ref[piece, slots] = facts


def pick_kernel(slots, pieces_ref, out_ref, facts_ref, facts, spots, sem):
    count = facts_ref.shape[0]
    for piece in range(count):
        tile = pieces_ref[piece * (slots + 1) + slots].astype(jnp.float32)
        facts_ref[piece:piece + 1] = tile.astype(jnp.int32)[0:1]
    copy = pltpu.make_async_copy(facts_ref, facts, sem)
    copy.start()
    copy.wait()
    for piece in range(count):
        for slot in range(slots):
            spots[facts[piece, slot]] = piece * (slots + 1) + slot

    def one(shot, carry):
        first = facts[shot, slots] * GRID_COLS + facts[shot, slots + 1]
        tiles = []
        for x in range(APX):
            for y in range(APY):
                tiles.append(pieces_ref[spots[first + x * GRID_COLS + y]])
        for index, tile in enumerate(tiles):
            out_ref[shot * APX * APY + index] = tile
        return carry

    lax.fori_loop(0, count, one, 0, unroll=4)


def ends(shape):
    lane = lax.broadcasted_iota(jnp.int32, shape, 1)
    row = lax.broadcasted_iota(jnp.int32, shape, 0)
    return lane == 0, lane == shape[1] - 1, row == 0, row == shape[0] - 1


def laplace(before, here, after, masks):
    lane_0, lane_n, row_0, row_n = masks
    many = len(here)
    depth = here[0].shape[1]
    low = [jnp.where(row_0, 0.0, pltpu.roll(here[-1], 1, 0))] + here[:-1]
    high = here[1:] + [jnp.where(row_n, 0.0, pltpu.roll(here[0], LANES - 1, 0))]
    result = []
    for v in range(many):
        up = jnp.where(lane_0, 0.0, pltpu.roll(here[v], 1, 1))
        down = jnp.where(lane_n, 0.0, pltpu.roll(here[v], depth - 1, 1))
        total = (before[v] + after[v]) + (low[v] + high[v]) + (up + down)
        result.append(total - 6.0 * here[v])
    return result


def registers(ref, x):
    return [ref[x, v] for v in range(ref.shape[1])]


def strided(ref, x):
    many = ref.shape[1] // LANES
    return [ref[x, pl.ds(v, LANES, stride=many)] for v in range(many)]


def sweep(count, fields, body, unroll):
    many = fields[0].shape[1]
    zero = [jnp.zeros(fields[0].shape[2:], jnp.float32)] * many
    first = [(zero, registers(field, 0)) for field in fields]

    def step(x, carry):
        rows = [
            (before, here, registers(field, x + 1))
            for (before, here), field in zip(carry, fields)
        ]
        body(x, rows)
        return [(here, after) for _, here, after in rows]

    lax.fori_loop(0, count, step, first, unroll=unroll)


def start_kernel(prev_ref, now_ref, wave_ref, grad_ref, next_ref, flat, flat_prev, field):
    span_x, span_y, depth = now_ref.shape
    many = span_y // LANES
    masks = ends((LANES, depth))

    def load(x, carry):
        flat[x] = now_ref[x].astype(jnp.float32)
        flat_prev[x] = prev_ref[x].astype(jnp.float32)
        return carry

    lax.fori_loop(0, span_x, load, 0, unroll=2)

    def order(x, carry):
        rows = strided(flat, x)
        older = strided(flat_prev, x)
        for v in range(many):
            field[x, v] = rows[v]
            wave_ref[x, v] = rows[v]
            next_ref[x, v] = 2.0 * rows[v] - older[v]
        return carry

    lax.fori_loop(0, span_x, order, 0, unroll=2)
    for v in range(many):
        field[span_x, v] = jnp.zeros((LANES, depth), jnp.float32)

    def body(x, rows):
        grads = laplace(*rows[0], masks)
        for v in range(many):
            grad_ref[x, v] = grads[v]

    sweep(span_x, [field], body, 8)


def start(before, current):
    span_x, span_y, depth = before.shape
    many = span_y // LANES
    out = jax.ShapeDtypeStruct((span_x, many, LANES, depth), jnp.float32)
    flat = pltpu.VMEM((span_x, span_y, depth), jnp.float32)
    return pl.pallas_call(
        start_kernel,
        out_shape=(out, out, out),
        in_specs=[vmem()] * 2,
        out_specs=(vmem(),) * 3,
        scratch_shapes=[flat, flat, pltpu.VMEM((span_x + 1, many, LANES, depth), jnp.float32)],
        compiler_params=pltpu.CompilerParams(vmem_limit_bytes=24 * 2**20),
        cost_estimate=pl.CostEstimate(
            flops=20 * before.size, bytes_accessed=16 * before.size, transcendentals=0
        ),
        name="start",
    )(before, current)


def wave_kernel(
    model_ref, u_0, g_0, next_ref, out_ref,
    kap, con, u_1, u_2, u_3, d_0, d_1, d_2, kb_3, kb_2, kb_1, g_1, g_2, d_3, b_2, b_1, image,
):
    span_x, many = u_0.shape[:2]
    depth = u_0.shape[3]
    block_y = model_ref.shape[2]
    block_x = span_x // APX
    masks = ends((LANES, depth))
    each = range(many)
    for field in (u_1, u_2, u_3, d_0, d_1, d_2, kb_3, kb_2, kb_1):
        for v in each:
            field[span_x, v] = jnp.zeros((LANES, depth), jnp.float32)

    def load(piece, carry):
        for x in range(APX):
            for y in range(APY):
                rows = pl.ds(y * block_y, block_y)
                at = x * block_x + piece
                kap[at, rows] = model_ref[2 * piece, x * APY + y].astype(jnp.float32)
                con[at, rows] = speed_factor * (
                    model_ref[2 * piece + 1, x * APY + y].astype(jnp.float32)
                )
        return carry

    lax.fori_loop(0, block_x, load, 0, unroll=4)

    def forward_0(x, carry):
        kaps, cons, grads = strided(kap, x), strided(con, x), registers(g_0, x)
        older = registers(next_ref, x)
        for v in each:
            d_0[x, v] = cons[v] * grads[v]
            u_1[x, v] = older[v] + kaps[v] * grads[v]
        return carry

    lax.fori_loop(0, span_x, forward_0, 0, unroll=8)

    def forward(u_now, u_prev, d_now, d_prev, u_next, d_next, g_now):
        def body(x, rows):
            waves, deltas = rows
            grads = laplace(*waves, masks)
            spread = laplace(*deltas, masks)
            kaps, cons = strided(kap, x), strided(con, x)
            for v in each:
                value = 2.0 * deltas[1][v] + kaps[v] * spread[v] + cons[v] * grads[v]
                if d_prev is not None:
                    value = value - d_prev[x, v]
                d_next[x, v] = value
                if u_next is None:
                    image[x, v] = grads[v] * value
                    kb_3[x, v] = kaps[v] * value
                else:
                    g_now[x, v] = grads[v]
                    u_next[x, v] = 2.0 * waves[1][v] - u_prev[x, v] + kaps[v] * grads[v]

        sweep(span_x, [u_now, d_now], body, 8)

    forward(u_1, u_0, d_0, None, u_2, d_1, g_1)
    forward(u_2, u_1, d_1, d_0, u_3, d_2, g_2)
    forward(u_3, u_2, d_2, d_1, None, d_3, None)

    def adjoint(kb, b_now, b_after, data, grad, kb_next, b_next):
        def body(x, rows):
            spread = laplace(*rows[0], masks)
            kaps = None if kb_next is None else strided(kap, x)
            for v in each:
                back = 2.0 * b_now[x, v] + spread[v] + data[x, v]
                if b_after is not None:
                    back = back - b_after[x, v]
                total = image[x, v] + grad[x, v] * back
                if kb_next is None:
                    total = (image_scale * total).astype(out_ref.dtype)
                    piece = 2 * (x % block_x) + v // 2
                    out_ref[piece, 2 * (x // block_x) + v % 2] = total
                else:
                    image[x, v] = total
                    b_next[x, v] = back
                    kb_next[x, v] = kaps[v] * back

        sweep(span_x, [kb], body, 8)

    adjoint(kb_3, d_3, None, d_2, g_2, kb_2, b_2)
    adjoint(kb_2, b_2, d_3, d_1, g_1, kb_1, b_1)
    adjoint(kb_1, b_1, b_2, d_0, g_0, None, None)


def wave(model, before, current):
    span_x, span_y, depth = before.shape
    pieces, blocks, block_y, _ = model.shape
    many = span_y // LANES
    flat = pltpu.VMEM((span_x, span_y, depth), jnp.float32)
    field = pltpu.VMEM((span_x + 1, many, LANES, depth), jnp.float32)
    plain = pltpu.VMEM((span_x, many, LANES, depth), jnp.float32)
    return pl.pallas_call(
        wave_kernel,
        out_shape=jax.ShapeDtypeStruct((pieces, blocks // 2, block_y, depth), jnp.bfloat16),
        in_specs=[vmem()] * 4,
        out_specs=vmem(),
        scratch_shapes=[flat] * 2 + [field] * 9 + [plain] * 6,
        compiler_params=pltpu.CompilerParams(vmem_limit_bytes=40 * 2**20),
        name="wave",
    )(model, *start(before, current))


def wave_split_depth(model, before, current):
    span_x, span_y, depth = before.shape
    pieces, blocks, block_y, _ = model.shape
    block_x = pieces // 2
    grids = model.reshape(block_x, 2, APX, APY, block_y, depth).transpose(1, 2, 0, 3, 4, 5)
    grids = grids.reshape(2, span_x, span_y, depth).astype(jnp.float32)
    image = image_scale * propagate(
        grids[0],
        speed_factor * grids[1],
        before.astype(jnp.float32),
        current.astype(jnp.float32),
        laplace_many,
    )
    many = span_y // LANES
    image = image.reshape(APX, block_x, LANES, 2, many // 2, depth).transpose(1, 3, 0, 4, 2, 5)
    return image.reshape(pieces, blocks // 2, block_y, depth).astype(jnp.bfloat16)


def stack_kernel(slots, facts_ref, terms_ref, out_ref, total, lined):
    shots, tiles = terms_ref.shape[:2]
    wide = tiles // APX
    width = LANES // APY
    long = width * wide
    grid_rows = total.shape[0] // wide
    depth = total.shape[2]

    def clear(index, carry):
        total[index] = jnp.zeros(total.shape[1:], total.dtype)
        return carry

    lax.fori_loop(0, total.shape[0], clear, 0, unroll=8)

    def add(shot, carry):
        first = facts_ref[shot, slots] * wide
        rows = pl.ds(facts_ref[shot, slots + 1] * width, LANES)
        sums = [
            total[first + tile, rows] + terms_ref[shot, tile].astype(jnp.float32)
            for tile in range(tiles)
        ]
        for tile in range(tiles):
            total[first + tile, rows] = sums[tile]
        return carry

    lax.fori_loop(0, shots, add, 0, unroll=2)

    for row in range(grid_rows):
        for part in range(wide):
            for tile in range(total.shape[1] // LANES):
                at = pl.ds(LANES + tile * LANES * wide + part, LANES, stride=wide)
                lined[row, at] = total[row * wide + part, tile * LANES:(tile + 1) * LANES]

    low = lax.broadcasted_iota(jnp.int32, (LANES, depth), 0) < long

    def window(owner, slot, shift):
        block = facts_ref[owner, slot]
        return lined[block // GRID_COLS, pl.ds(LANES - shift + block % GRID_COLS * long, LANES)]

    def give(owner, carry):
        pairs = [
            jnp.where(low, window(owner, slot, 0), window(owner, slot + 1, long))
            for slot in range(0, slots, 2)
        ]
        to = owner % NEAR * (shots // NEAR) + owner // NEAR
        out_ref[to] = jnp.concatenate(pairs, axis=0).astype(out_ref.dtype)
        return carry

    lax.fori_loop(0, shots, give, 0, unroll=4)


def finish_kernel(sums_ref, out_ref):
    slots, block_x = out_ref.shape[:2]
    depth = out_ref.shape[3]
    row = lax.broadcasted_iota(jnp.int32, (LANES, depth), 0)
    pair = row // 2
    for x in range(block_x):
        first = sums_ref[2 * x].astype(jnp.float32)
        second = sums_ref[2 * x + 1].astype(jnp.float32)
        for slot in range(slots):
            at = slot // 2 * LANES
            back = slot % 2 * (LANES // 2)
            one = first[at:at + LANES]
            two = second[at:at + LANES]

            def turned(value, shift):
                shift = (shift - back) % LANES
                return pltpu.roll(value, shift, 0) if shift else value

            result = jnp.where(pair == 0, turned(one, 0), turned(two, 2))
            result = jnp.where(pair == 2, turned(one, 2), result)
            out_ref[slot, x] = jnp.where(pair == 3, turned(two, 4), result)


def exchange(values):
    count = values.shape[0]
    far = count // NEAR
    inner = [[o * NEAR + i for i in range(NEAR)] for o in range(far)]
    outer = [[o * NEAR + i for o in range(far)] for i in range(NEAR)]
    values = lax.all_to_all(values, "shot", 0, 0, axis_index_groups=inner, tiled=True)
    values = values.reshape(NEAR, far, *values.shape[1:]).swapaxes(0, 1)
    values = values.reshape(count, *values.shape[2:])
    return lax.all_to_all(values, "shot", 0, 0, axis_index_groups=outer, tiled=True)


def per_device(
    velocity_p,
    velocity_s,
    density,
    perturbation,
    seafloor,
    owner_ids,
    corner_x,
    corner_y,
    wave_prev,
    wave_now,
):
    slots, block_x, block_y, depth = velocity_p.shape
    count = lax.axis_size("shot")
    assert count == 2 * block_x and block_y == LANES
    patch = APX * APY
    split = lax.axis_size("depth") > 1
    if split:
        seafloor = seafloor - lax.axis_index("depth") * depth

    sent = pl.pallas_call(
        prepare_kernel,
        out_shape=jax.ShapeDtypeStruct((count, slots + 1, block_y, depth), jnp.bfloat16),
        in_specs=[smem()] * 3 + [vmem()] * 5,
        out_specs=vmem(),
        name="prepare",
    )(owner_ids, corner_x, corner_y, seafloor, velocity_p, velocity_s, density, perturbation)
    pieces = lax.all_to_all(sent, "shot", 0, 0, tiled=True)

    picked, facts = pl.pallas_call(
        functools.partial(pick_kernel, slots),
        out_shape=(
            jax.ShapeDtypeStruct((count * patch, block_y, depth), jnp.bfloat16),
            jax.ShapeDtypeStruct((count, depth), jnp.int32),
        ),
        in_specs=[vmem()],
        out_specs=(vmem(), vmem()),
        scratch_shapes=[
            pltpu.SMEM((count, depth), jnp.int32),
            pltpu.SMEM((count * slots,), jnp.int32),
            pltpu.SemaphoreType.DMA,
        ],
        name="pick",
    )(pieces.reshape(count * (slots + 1), block_y, depth))
    model = lax.all_to_all(
        picked.reshape(count, patch, block_y, depth), "shot", 0, 0, tiled=True
    )

    run = wave_split_depth if split else wave
    terms = run(model, wave_prev[0], wave_now[0])
    terms = lax.all_to_all(terms, "shot", 0, 0, tiled=True)

    rows = block_x * block_y // count
    grid_rows = count * slots // GRID_COLS
    wide = terms.shape[1] // APX
    sums = pl.pallas_call(
        functools.partial(stack_kernel, slots),
        out_shape=jax.ShapeDtypeStruct((count, slots * rows, depth), jnp.bfloat16),
        in_specs=[smem(), vmem()],
        out_specs=vmem(),
        scratch_shapes=[
            pltpu.VMEM((grid_rows * wide, GRID_COLS * LANES // APY, depth), jnp.float32),
            pltpu.VMEM((grid_rows, 2 * LANES + GRID_COLS * rows, depth), jnp.float32),
        ],
        name="stack",
    )(facts, terms)
    sums = exchange(sums)
    return pl.pallas_call(
        finish_kernel,
        out_shape=jax.ShapeDtypeStruct(velocity_p.shape, jnp.float32),
        in_specs=[vmem()],
        out_specs=vmem(),
        name="finish",
    )(sums)


def solution(mesh):
    in_specs = (
        P(("grp", "shot"), None, None, "depth"),
        P(("grp", "shot"), None, None, "depth"),
        P(("grp", "shot"), None, None, "depth"),
        P(("grp", "shot"), None, None, "depth"),
        P(("grp", "shot"), None, None),
        P(("grp", "shot")),
        P(("grp", "shot")),
        P(("grp", "shot")),
        P(("grp", "shot"), None, None, "depth"),
        P(("grp", "shot"), None, None, "depth"),
    )
    out_specs = P(("grp", "shot"), None, None, "depth")
    return jax.shard_map(
        per_device, mesh=mesh, in_specs=in_specs, out_specs=out_specs, check_vma=False
    )
```

profile of v0, /device:TPU:0, one launch (start us, length us, event | category | flops | bytes accessed | tf_op | source)
XLA Modules:
  0.0 78.3 jit_solution(3874703698886671887)
XLA Ops:
  1.3 1.7 %prepare.1 = bf16[16,5,8,128]{3,2,1,0:T(8,128)(2,1)} custom-call(s32[4]{0:T(128)} %ids_ref.1, s32[1]{0:T(128)S(6)} %copy.12.row_ref, s32[1]{0:T(128)S(6)} %copy.13.col_ref, s32[4,8,8]{2,1,0:T(8,128)} %floor_ref.1, bf16[4,8,8,128]{3,2,1,0:T(8,128)(2,1)} %p_ref.1, bf16[4,8,8,128]{3,2,1,0:T(8,128)(2,1)} %s_ref.1, bf16[4,8,8,128]{3,2,1,0:T(8,128)(2,1)} %rho_ref.1, ...), custom_call_target="tpu_custom_call" | custom-call | tf_op jit(solution)/shard_map/prepare/pallas_call | solution.py:462
  3.0 15.9 %all_to_all.25 = bf16[16,5,8,128]{3,2,1,0:T(8,128)(2,1)} all-to-all(bf16[16,5,8,128]{3,2,1,0:T(8,128)(2,1)} %prepare.1), channel_id=1, replica_groups=mesh['grp'=2,'shot'=16,'depth'=1] {'shot'}, dimensions={0} | all-to-all | bytes 327680 | tf_op jit(solution)/shard_map/all_to_all | solution.py:469
  19.0 2.8 %pick.1 = (bf16[256,8,128]{2,1,0:T(8,128)(2,1)}, s32[16,128]{1,0:T(8,128)}) custom-call(bf16[80,8,128]{2,1,0:T(8,128)(2,1)} %bitcast.10), custom_call_target="tpu_custom_call" | custom-call | tf_op jit(solution)/shard_map/pick/pallas_call | solution.py:471
  21.8 0.0 copy-start
  21.8 0.0 copy-start.1
  21.8 3.7 %all-to-all-start.1 = ((bf16[16,16,8,128]{3,2,1,0:T(8,128)(2,1)}), bf16[16,16,8,128]{3,2,1,0:T(8,128)(2,1)S(1)}, u32[]{:S(2)}, u32[]{:S(2)}) async-start(bf16[16,16,8,128]{3,2,1,0:T(8,128)(2,1)} %bitcast.11), calls=%async_computation.1 | async-start | bytes 1048576 | tf_op jit(solution)/shard_map/all_to_all | solution.py:486
  25.5 0.0 copy-done
  25.5 0.0 copy-done.1
  25.5 0.8 %start.1 = (f32[32,4,8,128]{3,2,1,0:T(8,128)S(1)}, f32[32,4,8,128]{3,2,1,0:T(8,128)S(1)}, f32[32,4,8,128]{3,2,1,0:T(8,128)S(1)}) custom-call(bf16[32,32,128]{2,1,0:T(8,128)(2,1)S(1)} %bitcast.8, bf16[32,32,128]{2,1,0:T(8,128)(2,1)S(1)} %bitcast.9), custom_call_target="tpu_custom_call" | custom-call | flops 2621440 | bytes 2097152 | tf_op jit(solution)/shard_map/start/pallas_call | solution.py:221
  26.4 13.6 %all-to-all-done.1.model_ref = bf16[16,16,8,128]{3,2,1,0:T(8,128)(2,1)S(1)} async-done(((bf16[16,16,8,128]{3,2,1,0:T(8,128)(2,1)}), bf16[16,16,8,128]{3,2,1,0:T(8,128)(2,1)S(1)}, u32[]{:S(2)}, u32[]{:S(2)}) %all-to-all-start.1) | async-done | bytes 524320 | tf_op jit(solution)/shard_map/all_to_all | solution.py:486
  39.9 4.4 %wave.1 = bf16[16,8,8,128]{3,2,1,0:T(8,128)(2,1)S(1)} custom-call(bf16[16,16,8,128]{3,2,1,0:T(8,128)(2,1)S(1)} %all-to-all-done.1.model_ref, f32[32,4,8,128]{3,2,1,0:T(8,128)S(1)} %get-tuple-element.12.u_0, f32[32,4,8,128]{3,2,1,0:T(8,128)S(1)} %get-tuple-element.13.g_0, f32[32,4,8,128]{3,2,1,0:T(8,128)S(1)} %get-tuple-element.14.next_ref), custom_call_target="tpu_custom_call" | custom-call | tf_op jit(solution)/shard_map/wave/pallas_call | solution.py:328
  44.4 14.0 %all_to_all.26.terms_ref = bf16[16,8,8,128]{3,2,1,0:T(8,128)(2,1)} all-to-all(bf16[16,8,8,128]{3,2,1,0:T(8,128)(2,1)S(1)} %wave.1), channel_id=1, replica_groups=mesh['grp'=2,'shot'=16,'depth'=1] {'shot'}, dimensions={0} | all-to-all | bytes 524288 | tf_op jit(solution)/shard_map/all_to_all | solution.py:492
  58.3 2.3 %stack.1 = bf16[16,16,128]{2,1,0:T(8,128)(2,1)} custom-call(s32[16,128]{1,0:T(8,128)} %get-tuple-element.10.facts_ref, bf16[16,8,8,128]{3,2,1,0:T(8,128)(2,1)} %all_to_all.26.terms_ref), custom_call_target="tpu_custom_call" | custom-call | tf_op jit(solution)/shard_map/stack/pallas_call | solution.py:497
  60.6 7.4 %all_to_all.27 = bf16[16,16,128]{2,1,0:T(8,128)(2,1)S(1)} all-to-all(bf16[16,16,128]{2,1,0:T(8,128)(2,1)} %stack.1), channel_id=1, replica_groups={{0,1,2,3},{4,5,6,7},{8,9,10,11},{12,13,14,15},{16,17,18,19},{20,21,22,2..., dimensions={0} | all-to-all | bytes 131072 | tf_op jit(solution)/shard_map/all_to_all | solution.py:436
  68.0 8.8 %all_to_all.28.sums_ref = bf16[16,16,128]{2,1,0:T(8,128)(2,1)} all-to-all(bf16[16,16,128]{2,1,0:T(8,128)(2,1)S(1)} %bitcast.13), channel_id=1, replica_groups={{0,4,8,12},{1,5,9,13},{2,6,10,14},{3,7,11,15},{16,20,24,28},{17,21,25,2..., dimensions={0} | all-to-all | bytes 131072 | tf_op jit(solution)/shard_map/all_to_all | solution.py:439
  76.7 1.5 %finish.1 = f32[4,8,8,128]{3,2,1,0:T(8,128)} custom-call(bf16[16,16,128]{2,1,0:T(8,128)(2,1)} %all_to_all.28.sums_ref), custom_call_target="tpu_custom_call" | custom-call | tf_op jit(solution)/shard_map/finish/pallas_call | solution.py:509
  (1 shorter events, 0.0 us)
Async XLA Ops:
  21.8 3.7 %copy-start = (bf16[1,32,32,128]{3,2,1,0:T(8,128)(2,1)S(1)}, bf16[1,32,32,128]{3,2,1,0:T(8,128)(2,1)}, u32[]{:S(2)}) copy-start(bf16[1,32,32,128]{3,2,1,0:T(8,128)(2,1)} %param.18) | copy-start | bytes 786436
  21.8 3.7 %copy-start.1 = (bf16[1,32,32,128]{3,2,1,0:T(8,128)(2,1)S(1)}, bf16[1,32,32,128]{3,2,1,0:T(8,128)(2,1)}, u32[]{:S(2)}) copy-start(bf16[1,32,32,128]{3,2,1,0:T(8,128)(2,1)} %param.19) | copy-start | bytes 786436
  21.8 18.1 %all-to-all-start.1 = ((bf16[16,16,8,128]{3,2,1,0:T(8,128)(2,1)}), bf16[16,16,8,128]{3,2,1,0:T(8,128)(2,1)S(1)}, u32[]{:S(2)}, u32[]{:S(2)}) async-start(bf16[16,16,8,128]{3,2,1,0:T(8,128)(2,1)} %bitcast.11), calls=%async_computation.1 | async-start | bytes 1048576 | tf_op jit(solution)/shard_map/all_to_all | solution.py:486
where the time goes:
time: 78.9 us; the launch traced here: 78.3 us
  blocking collectives  46 us (58%)
  Pallas kernels  13.6 us (17%)
  waiting for transfers between devices  13.6 us (17%)
  starting transfers between devices  3.71 us (5%)
  between operations  1.36 us (2%)
    all_to_all x1, blocking collectives, per_device(): pieces = lax.all_to_all(sent, 'shot', 0, 0, tiled=True)  15.9 us
    all_to_all x1, blocking collectives, per_device(): terms = lax.all_to_all(terms, 'shot', 0, 0, tiled=True)  14 us
    all_to_all x1, waiting for transfers between devices, per_device(): lax.all_to_all(picked.reshape(count, patch, block_y, depth), 'shot', 0, 0...  13.6 us
    all_to_all x1, blocking collectives, exchange(): lax.all_to_all(values, 'shot', 0, 0, axis_index_groups=outer, tiled=True)  8.77 us
    all_to_all x1, blocking collectives, exchange(): lax.all_to_all(values, 'shot', 0, 0, axis_index_groups=inner, tiled=True)  7.37 us
    pallas_call x1, Pallas kernels, wave(): pl.pallas_call(wave_kernel, out_shape=jax.ShapeDtypeStruct((pieces, block...  4.43 us
    all_to_all x1, starting transfers between devices, per_device(): lax.all_to_all(picked.reshape(count, patch, block_y, depth), 'shot', 0, 0...  3.71 us
    pallas_call x1, Pallas kernels, per_device(): pl.pallas_call(functools.partial(pick_kernel, slots), out_shape=(jax.Shap...  2.79 us
  transfers between devices with their start and end apart: 1, of which 1 were waited for; matrix products, arithmetic and copies ran while one was open for 0% of the time, Pallas kernels for 1%

commit v1 on v0

--- a/solution.py
+++ b/solution.py
@@ -11,7 +11,6 @@
 APY = 4
 STEPS = 4
 GRID_COLS = 8
-NEAR = 4
 LANES = 8
 
 speed_factor = 0.28
@@ -70,6 +69,10 @@
     return image
 
 
+def limit(mebibytes):
+    return pltpu.CompilerParams(vmem_limit_bytes=mebibytes * 2**20)
+
+
 def vmem():
     return pl.BlockSpec(memory_space=pltpu.VMEM)
 
@@ -79,7 +82,7 @@
 
 
 def prepare_kernel(
-    ids_ref, row_ref, col_ref, floor_ref, p_ref, s_ref, rho_ref, pert_ref, out_ref
+    ids_ref, row_ref, col_ref, floor_ref, p_ref, s_ref, rho_ref, pert_ref, out_ref, lined
 ):
     slots, block_x, block_y, depth = p_ref.shape
     shape = (block_y, depth)
@@ -99,11 +102,11 @@
             coef = speed_factor * stiffness / rho_ref[slot, x].astype(jnp.float32)
             out_ref[2 * x, slot] = coef.astype(out_ref.dtype)
             out_ref[2 * x + 1, slot] = pert_ref[slot, x]
+    lined[...] = jnp.zeros(shape, jnp.int32)
+    lined[0:1, 0:slots] = ids_ref[...]
     lane = lax.broadcasted_iota(jnp.int32, shape, 1)
-    facts = jnp.where(lane == slots, row_ref[0], 0)
+    facts = jnp.where(lane == slots, row_ref[0], lined[...])
     facts = jnp.where(lane == slots + 1, col_ref[0], facts)
-    for slot in range(slots):
-        facts = jnp.where(lane == slot, ids_ref[slot], facts)
     facts = facts.astype(jnp.float32).astype(out_ref.dtype)
     for piece in range(out_ref.shape[0]):
         out_ref[piece, slots] = facts
@@ -224,7 +227,7 @@
         in_specs=[vmem()] * 2,
         out_specs=(vmem(),) * 3,
         scratch_shapes=[flat, flat, pltpu.VMEM((span_x + 1, many, LANES, depth), jnp.float32)],
-        compiler_params=pltpu.CompilerParams(vmem_limit_bytes=24 * 2**20),
+        compiler_params=limit(8),
         cost_estimate=pl.CostEstimate(
             flops=20 * before.size, bytes_accessed=16 * before.size, transcendentals=0
         ),
@@ -331,7 +334,7 @@
         in_specs=[vmem()] * 4,
         out_specs=vmem(),
         scratch_shapes=[flat] * 2 + [field] * 9 + [plain] * 6,
-        compiler_params=pltpu.CompilerParams(vmem_limit_bytes=40 * 2**20),
+        compiler_params=limit(20),
         name="wave",
     )(model, *start(before, current))
 
@@ -354,23 +357,26 @@
     return image.reshape(pieces, blocks // 2, block_y, depth).astype(jnp.bfloat16)
 
 
-def stack_kernel(slots, facts_ref, terms_ref, out_ref, total, lined):
+def stack_kernel(slots, facts_ref, terms_ref, out_ref, facts, total, lined, sem):
     shots, tiles = terms_ref.shape[:2]
     wide = tiles // APX
     width = LANES // APY
     long = width * wide
     grid_rows = total.shape[0] // wide
     depth = total.shape[2]
+    copy = pltpu.make_async_copy(facts_ref, facts, sem)
+    copy.start()
 
     def clear(index, carry):
         total[index] = jnp.zeros(total.shape[1:], total.dtype)
         return carry
 
     lax.fori_loop(0, total.shape[0], clear, 0, unroll=8)
+    copy.wait()
 
     def add(shot, carry):
-        first = facts_ref[shot, slots] * wide
-        rows = pl.ds(facts_ref[shot, slots + 1] * width, LANES)
+        first = facts[shot, slots] * wide
+        rows = pl.ds(facts[shot, slots + 1] * width, LANES)
         sums = [
             total[first + tile, rows] + terms_ref[shot, tile].astype(jnp.float32)
             for tile in range(tiles)
@@ -390,7 +396,7 @@
     low = lax.broadcasted_iota(jnp.int32, (LANES, depth), 0) < long
 
     def window(owner, slot, shift):
-        block = facts_ref[owner, slot]
+        block = facts[owner, slot]
         return lined[block // GRID_COLS, pl.ds(LANES - shift + block % GRID_COLS * long, LANES)]
 
     def give(owner, carry):
@@ -398,8 +404,7 @@
             jnp.where(low, window(owner, slot, 0), window(owner, slot + 1, long))
             for slot in range(0, slots, 2)
         ]
-        to = owner % NEAR * (shots // NEAR) + owner // NEAR
-        out_ref[to] = jnp.concatenate(pairs, axis=0).astype(out_ref.dtype)
+        out_ref[owner] = jnp.concatenate(pairs, axis=0).astype(out_ref.dtype)
         return carry
 
     lax.fori_loop(0, shots, give, 0, unroll=4)
@@ -426,17 +431,6 @@
             result = jnp.where(pair == 0, turned(one, 0), turned(two, 2))
             result = jnp.where(pair == 2, turned(one, 2), result)
             out_ref[slot, x] = jnp.where(pair == 3, turned(two, 4), result)
-
-
-def exchange(values):
-    count = values.shape[0]
-    far = count // NEAR
-    inner = [[o * NEAR + i for i in range(NEAR)] for o in range(far)]
-    outer = [[o * NEAR + i for o in range(far)] for i in range(NEAR)]
-    values = lax.all_to_all(values, "shot", 0, 0, axis_index_groups=inner, tiled=True)
-    values = values.reshape(NEAR, far, *values.shape[1:]).swapaxes(0, 1)
-    values = values.reshape(count, *values.shape[2:])
-    return lax.all_to_all(values, "shot", 0, 0, axis_index_groups=outer, tiled=True)
 
 
 def per_device(
@@ -462,10 +456,15 @@
     sent = pl.pallas_call(
         prepare_kernel,
         out_shape=jax.ShapeDtypeStruct((count, slots + 1, block_y, depth), jnp.bfloat16),
-        in_specs=[smem()] * 3 + [vmem()] * 5,
+        in_specs=[vmem()] + [smem()] * 2 + [vmem()] * 5,
         out_specs=vmem(),
+        scratch_shapes=[pltpu.VMEM((block_y, depth), jnp.int32)],
+        compiler_params=limit(2),
         name="prepare",
-    )(owner_ids, corner_x, corner_y, seafloor, velocity_p, velocity_s, density, perturbation)
+    )(
+        owner_ids[None], corner_x, corner_y, seafloor,
+        velocity_p, velocity_s, density, perturbation,
+    )
     pieces = lax.all_to_all(sent, "shot", 0, 0, tiled=True)
 
     picked, facts = pl.pallas_call(
@@ -481,6 +480,7 @@
             pltpu.SMEM((count * slots,), jnp.int32),
             pltpu.SemaphoreType.DMA,
         ],
+        compiler_params=limit(3),
         name="pick",
     )(pieces.reshape(count * (slots + 1), block_y, depth))
     model = lax.all_to_all(
@@ -497,20 +497,24 @@
     sums = pl.pallas_call(
         functools.partial(stack_kernel, slots),
         out_shape=jax.ShapeDtypeStruct((count, slots * rows, depth), jnp.bfloat16),
-        in_specs=[smem(), vmem()],
+        in_specs=[vmem(), vmem()],
         out_specs=vmem(),
         scratch_shapes=[
+            pltpu.SMEM(facts.shape, jnp.int32),
             pltpu.VMEM((grid_rows * wide, GRID_COLS * LANES // APY, depth), jnp.float32),
             pltpu.VMEM((grid_rows, 2 * LANES + GRID_COLS * rows, depth), jnp.float32),
+            pltpu.SemaphoreType.DMA,
         ],
+        compiler_params=limit(3),
         name="stack",
     )(facts, terms)
-    sums = exchange(sums)
+    sums = lax.all_to_all(sums, "shot", 0, 0, tiled=True)
     return pl.pallas_call(
         finish_kernel,
         out_shape=jax.ShapeDtypeStruct(velocity_p.shape, jnp.float32),
         in_specs=[vmem()],
         out_specs=vmem(),
+        compiler_params=limit(2),
         name="finish",
     )(sums)
 

time: 78.9 us -> 72.3 us (0.916)
  blocking collectives: 46 us -> 39.2 us
  local copies, waits for them, and re-layouts: 0.02 us -> 4.73 us
  Pallas kernels: 13.6 us -> 9.19 us
    all_to_all x2 -> x1, blocking collectives: 16.1 us -> 9.67 us  [per_device(): sums = lax.all_to_all(sums, 'shot', 0, 0, tiled=True)]
    unnamed x4 -> x16, local copies, waits for them, and re-layouts: 0.01 us -> 4.73 us
    pallas_call x1, Pallas kernels: 1.74 us -> 0.12 us  [per_device(): pl.pallas_call(prepare_kernel, out_shape=jax.ShapeDtypeStruct((count, slo...]
    pallas_call x1, Pallas kernels: 2.26 us -> 1.24 us  [per_device(): pl.pallas_call(functools.partial(stack_kernel, slots), out_shape=jax.Shap...]
    pallas_call x1, Pallas kernels: 2.79 us -> 1.88 us  [per_device(): pl.pallas_call(functools.partial(pick_kernel, slots), out_shape=(jax.Shap...]
    pallas_call x1, Pallas kernels: 1.53 us -> 0.69 us  [per_device(): pl.pallas_call(finish_kernel, out_shape=jax.ShapeDtypeStruct(velocity_p.s...]
where the time goes in v1:
time: 72.3 us; the launch traced here: 71.7 us
  blocking collectives  39.2 us (54%)
  waiting for transfers between devices  13.6 us (19%)
  Pallas kernels  9.19 us (13%)
  local copies, waits for them, and re-layouts  4.73 us (7%)
  starting transfers between devices  3.71 us (5%)
  between operations  1.39 us (2%)
    all_to_all x1, blocking collectives, per_device(): pieces = lax.all_to_all(sent, 'shot', 0, 0, tiled=True)  15.6 us
    all_to_all x1, blocking collectives, per_device(): terms = lax.all_to_all(terms, 'shot', 0, 0, tiled=True)  13.9 us
    all_to_all x1, waiting for transfers between devices, per_device(): lax.all_to_all(picked.reshape(count, patch, block_y, depth), 'shot', 0, 0...  13.6 us
    all_to_all x1, blocking collectives, per_device(): sums = lax.all_to_all(sums, 'shot', 0, 0, tiled=True)  9.67 us
    unnamed x16, local copies, waits for them, and re-layouts  4.73 us
    pallas_call x1, Pallas kernels, wave(): pl.pallas_call(wave_kernel, out_shape=jax.ShapeDtypeStruct((pieces, block...  4.43 us
    all_to_all x1, starting transfers between devices, per_device(): lax.all_to_all(picked.reshape(count, patch, block_y, depth), 'shot', 0, 0...  3.71 us
    pallas_call x1, Pallas kernels, per_device(): pl.pallas_call(functools.partial(pick_kernel, slots), out_shape=(jax.Shap...  1.88 us
  transfers between devices with their start and end apart: 1, of which 1 were waited for; matrix products, arithmetic and copies ran while one was open for 0% of the time, Pallas kernels for 1%

profile of v1, /device:TPU:0, one launch (start us, length us, event | category | flops | bytes accessed | tf_op | source)
XLA Modules:
  0.0 71.7 jit_solution(10258690803269313359)
XLA Ops:
  1.3 0.0 copy-start.7
  1.3 0.6 copy-done.7
  2.0 0.0 copy-start.2
  2.0 0.8 %copy-done.2 = bf16[4,8,8,128]{3,2,1,0:T(8,128)(2,1)S(1)} copy-done((bf16[4,8,8,128]{3,2,1,0:T(8,128)(2,1)S(1)}, bf16[4,8,8,128]{3,2,1,0:T(8,128)(2,1)}, u32[]{:S(2)}) %copy-start.2) | copy-done | bytes 65560
  2.8 0.0 copy-start.3
  2.8 0.8 %copy-done.3 = bf16[4,8,8,128]{3,2,1,0:T(8,128)(2,1)S(1)} copy-done((bf16[4,8,8,128]{3,2,1,0:T(8,128)(2,1)S(1)}, bf16[4,8,8,128]{3,2,1,0:T(8,128)(2,1)}, u32[]{:S(2)}) %copy-start.3) | copy-done | bytes 65560
  3.6 0.0 copy-start.4
  3.6 0.8 %copy-done.4 = bf16[4,8,8,128]{3,2,1,0:T(8,128)(2,1)S(1)} copy-done((bf16[4,8,8,128]{3,2,1,0:T(8,128)(2,1)S(1)}, bf16[4,8,8,128]{3,2,1,0:T(8,128)(2,1)}, u32[]{:S(2)}) %copy-start.4) | copy-done | bytes 65560
  4.5 0.0 copy-start.5
  4.5 0.8 %copy-done.5 = bf16[4,8,8,128]{3,2,1,0:T(8,128)(2,1)S(1)} copy-done((bf16[4,8,8,128]{3,2,1,0:T(8,128)(2,1)S(1)}, bf16[4,8,8,128]{3,2,1,0:T(8,128)(2,1)}, u32[]{:S(2)}) %copy-start.5) | copy-done | bytes 65560
  5.3 0.0 copy-start.6
  5.3 0.7 copy-done.6
  6.0 0.1 prepare.1
  6.2 15.6 %all_to_all.20 = bf16[16,5,8,128]{3,2,1,0:T(8,128)(2,1)S(1)} all-to-all(bf16[16,5,8,128]{3,2,1,0:T(8,128)(2,1)S(1)} %prepare.1), channel_id=1, replica_groups=mesh['grp'=2,'shot'=16,'depth'=1] {'shot'}, dimensions={0} | all-to-all | bytes 327680 | tf_op jit(solution)/shard_map/all_to_all | solution.py:468
  21.8 1.9 %pick.1 = (bf16[256,8,128]{2,1,0:T(8,128)(2,1)}, s32[16,128]{1,0:T(8,128)S(1)}) custom-call(bf16[80,8,128]{2,1,0:T(8,128)(2,1)S(1)} %bitcast.5), custom_call_target="tpu_custom_call" | custom-call | tf_op jit(solution)/shard_map/pick/pallas_call | solution.py:470
  23.7 0.0 copy-start
  23.7 0.0 copy-start.1
  23.7 3.7 %all-to-all-start.1 = ((bf16[16,16,8,128]{3,2,1,0:T(8,128)(2,1)}), bf16[16,16,8,128]{3,2,1,0:T(8,128)(2,1)S(1)}, u32[]{:S(2)}, u32[]{:S(2)}) async-start(bf16[16,16,8,128]{3,2,1,0:T(8,128)(2,1)} %bitcast.2), calls=%async_computation.1 | async-start | bytes 1048576 | tf_op jit(solution)/shard_map/all_to_all | solution.py:486
  27.4 0.0 copy-done
  27.4 0.0 copy-done.1
  27.4 0.8 %start.1 = (f32[32,4,8,128]{3,2,1,0:T(8,128)S(1)}, f32[32,4,8,128]{3,2,1,0:T(8,128)S(1)}, f32[32,4,8,128]{3,2,1,0:T(8,128)S(1)}) custom-call(bf16[32,32,128]{2,1,0:T(8,128)(2,1)S(1)} %bitcast.6, bf16[32,32,128]{2,1,0:T(8,128)(2,1)S(1)} %bitcast.7), custom_call_target="tpu_custom_call" | custom-call | flops 2621440 | bytes 2097152 | tf_op jit(solution)/shard_map/start/pallas_call | solution.py:224
  28.3 13.6 %all-to-all-done.1.model_ref = bf16[16,16,8,128]{3,2,1,0:T(8,128)(2,1)S(1)} async-done(((bf16[16,16,8,128]{3,2,1,0:T(8,128)(2,1)}), bf16[16,16,8,128]{3,2,1,0:T(8,128)(2,1)S(1)}, u32[]{:S(2)}, u32[]{:S(2)}) %all-to-all-start.1) | async-done | bytes 524320 | tf_op jit(solution)/shard_map/all_to_all | solution.py:486
  41.8 4.4 %wave.1 = bf16[16,8,8,128]{3,2,1,0:T(8,128)(2,1)S(1)} custom-call(bf16[16,16,8,128]{3,2,1,0:T(8,128)(2,1)S(1)} %all-to-all-done.1.model_ref, f32[32,4,8,128]{3,2,1,0:T(8,128)S(1)} %get-tuple-element.12.u_0, f32[32,4,8,128]{3,2,1,0:T(8,128)S(1)} %get-tuple-element.13.g_0, f32[32,4,8,128]{3,2,1,0:T(8,128)S(1)} %get-tuple-element.14.next_ref), custom_call_target="tpu_custom_call" | custom-call | tf_op jit(solution)/shard_map/wave/pallas_call | solution.py:331
  46.3 13.9 %all_to_all.21.terms_ref = bf16[16,8,8,128]{3,2,1,0:T(8,128)(2,1)S(1)} all-to-all(bf16[16,8,8,128]{3,2,1,0:T(8,128)(2,1)S(1)} %wave.1), channel_id=1, replica_groups=mesh['grp'=2,'shot'=16,'depth'=1] {'shot'}, dimensions={0} | all-to-all | bytes 524288 | tf_op jit(solution)/shard_map/all_to_all | solution.py:492
  60.1 1.2 %stack.1 = bf16[16,16,128]{2,1,0:T(8,128)(2,1)S(1)} custom-call(s32[16,128]{1,0:T(8,128)S(1)} %get-tuple-element.10.facts_ref, bf16[16,8,8,128]{3,2,1,0:T(8,128)(2,1)S(1)} %all_to_all.21.terms_ref), custom_call_target="tpu_custom_call" | custom-call | tf_op jit(solution)/shard_map/stack/pallas_call | solution.py:497
  61.4 9.7 %all_to_all.22.sums_ref = bf16[16,16,128]{2,1,0:T(8,128)(2,1)S(1)} all-to-all(bf16[16,16,128]{2,1,0:T(8,128)(2,1)S(1)} %stack.1), channel_id=1, replica_groups=mesh['grp'=2,'shot'=16,'depth'=1] {'shot'}, dimensions={0} | all-to-all | bytes 131072 | tf_op jit(solution)/shard_map/all_to_all | solution.py:511
  71.1 0.7 finish.1
Async XLA Ops:
  1.3 0.7 copy-start.7
  2.0 0.8 %copy-start.2 = (bf16[4,8,8,128]{3,2,1,0:T(8,128)(2,1)S(1)}, bf16[4,8,8,128]{3,2,1,0:T(8,128)(2,1)}, u32[]{:S(2)}) copy-start(bf16[4,8,8,128]{3,2,1,0:T(8,128)(2,1)} %p_ref.1) | copy-start | bytes 196612
  2.8 0.8 %copy-start.3 = (bf16[4,8,8,128]{3,2,1,0:T(8,128)(2,1)S(1)}, bf16[4,8,8,128]{3,2,1,0:T(8,128)(2,1)}, u32[]{:S(2)}) copy-start(bf16[4,8,8,128]{3,2,1,0:T(8,128)(2,1)} %s_ref.1) | copy-start | bytes 196612
  3.6 0.8 %copy-start.4 = (bf16[4,8,8,128]{3,2,1,0:T(8,128)(2,1)S(1)}, bf16[4,8,8,128]{3,2,1,0:T(8,128)(2,1)}, u32[]{:S(2)}) copy-start(bf16[4,8,8,128]{3,2,1,0:T(8,128)(2,1)} %rho_ref.1) | copy-start | bytes 196612
  4.5 0.8 %copy-start.5 = (bf16[4,8,8,128]{3,2,1,0:T(8,128)(2,1)S(1)}, bf16[4,8,8,128]{3,2,1,0:T(8,128)(2,1)}, u32[]{:S(2)}) copy-start(bf16[4,8,8,128]{3,2,1,0:T(8,128)(2,1)} %pert_ref.1) | copy-start | bytes 196612
  5.3 0.7 copy-start.6
  23.7 3.7 %copy-start = (bf16[1,32,32,128]{3,2,1,0:T(8,128)(2,1)S(1)}, bf16[1,32,32,128]{3,2,1,0:T(8,128)(2,1)}, u32[]{:S(2)}) copy-start(bf16[1,32,32,128]{3,2,1,0:T(8,128)(2,1)} %param.18) | copy-start | bytes 786436
  23.7 3.7 %copy-start.1 = (bf16[1,32,32,128]{3,2,1,0:T(8,128)(2,1)S(1)}, bf16[1,32,32,128]{3,2,1,0:T(8,128)(2,1)}, u32[]{:S(2)}) copy-start(bf16[1,32,32,128]{3,2,1,0:T(8,128)(2,1)} %param.19) | copy-start | bytes 786436
  23.7 18.1 %all-to-all-start.1 = ((bf16[16,16,8,128]{3,2,1,0:T(8,128)(2,1)}), bf16[16,16,8,128]{3,2,1,0:T(8,128)(2,1)S(1)}, u32[]{:S(2)}, u32[]{:S(2)}) async-start(bf16[16,16,8,128]{3,2,1,0:T(8,128)(2,1)} %bitcast.2), calls=%async_computation.1 | async-start | bytes 1048576 | tf_op jit(solution)/shard_map/all_to_all | solution.py:486
